TPU v7x, 512 devices: a whole 4x8x8 slice. The times are simulated.
512 devices in a mesh: dp: 4 (over x), row: 8 (over y), col: 16 (over z, core).
Axes of the slice: x: 4, y: 8, z: 8, core: 2. Of those that a mesh axis runs over, the one named last changes fastest.
Arguments:
- tokens: bfloat16 [2048, 8192], P('dp', ('row', 'col')), may hold values from -6 to 6
- weight_codes: bfloat16 [8192, 26624], P('row', 'col'), may hold values from -0.0625 to 0.0625
- group_scales: bfloat16 [64, 26624], P('row', 'col'), may hold values from 0.25 to 4
- adapter_down: bfloat16 [8192, 64], P('row'), may hold values from -0.0625 to 0.0625
- adapter_up: bfloat16 [64, 26624], P(None, 'col'), may hold values from -0.75 to 0.75
- up_branch: bfloat16 [2048, 26624], P(('dp', 'row'), 'col'), may hold values from -6 to 6
- hidden_grad: bfloat16 [2048, 26624], P(('dp', 'row'), 'col'), may hold values from -6 to 6
Outputs:
- grad_tokens: bfloat16 [2048, 8192], P('dp', ('row', 'col'))
- grad_down: float32 [8192, 64], P('row', 'col')
- grad_up: float32 [64, 26624], P(None, 'col')
All inputs are finite; a program needn't handle non-finite values.
Results may differ from a plain program's by a relative error of at most 0.034.
Values may be sent and summed in bfloat16 or wider, within the bound.
A program may use at most 64 MiB of HBM per device.

v0:
```python
import jax
import jax.numpy as jnp
from jax import lax
from jax.experimental import pallas as pl
from jax.experimental.pallas import tpu as pltpu
from jax.sharding import PartitionSpec as P

MESH = pl.DeviceIdType.MESH
NX, NY, NZ = 4, 8, 8
OWN = 64
PD = 64
D = NZ * 2 * PD
F = 1664
R = 64
CHUNKS = ((0, 256), (256, 768), (768, 1280), (1280, 1536), (1536, 1664))
Q = len(CHUNKS)
RS_ORDER = (4, 0, 1, 2, 3)
TWO = 3
SPLIT = CHUNKS[TWO][0]
GROUPS = ((0, 1, 7), (2, 6), (3, 5), (4,))
PEERS = (4, 3, 5, 2, 6, 1, 7)
f32 = jnp.float32
bf16 = jnp.bfloat16
NT = (((1,), (1,)), ((), ()))


def block_of(rel):
    if rel in (4, 0):
        return 0, 0 if rel == 4 else 1
    return (4 - rel, 0) if rel < 4 else (rel - 4, 1)


def kernel(
    tok_hbm, codes_hbm, scale_hbm, down_hbm, up_hbm, ub_hbm, hg_hbm,
    out_ref, gd_ref, gu_ref,
    tok_ref, codes, scale_ref, down_ref, up_ref, ub, hg, scale, W, WA, G, PK, xt, part, part_a,
    rs_snd, rs_rcv, a_snd, a_rcv, GR, GA, GB, a_all, back, bk_snd, bk_rcv, bz_snd, bz_rcv, by_snd, by_rcv, zfin,
    at_ref, up_acc, up_all, xs_snd, xs_rcv, xg_snd, xg_rcv, gd_all,
    *rest,
):
    group_bufs, sems = rest[: 4 * 6], rest[4 * 6 :]
    (loc_sem, tok_s, tok_r, sib_s, sib_r, rs_s, rs_r, ag_s, ag_r,
     ra_s, ra_r, ga_s, ga_r, ab_s, ab_r,
     p_s, p_r, z_s, z_r, bp_s, bp_r, bz_s, bz_r, by_s, by_r, xs_s, xs_r, xg_s, xg_r, gd_s, gd_r) = sems
    x = lax.axis_index("dp")
    y = lax.axis_index("row")
    col = lax.axis_index("col")
    z = col // 2
    c = lax.rem(col, 2)
    sib = {"col": 2 * z + 1 - c}

    def yid(k):
        return {"row": lax.rem(y + k + NY, NY)}

    def zid(k):
        return {"col": 2 * lax.rem(z + k, NZ) + c}

    def xid(k):
        return {"dp": lax.rem(x + k, NX)}

    def owner(rel):
        return lax.rem(y + rel, NY)

    sent = []

    def drain(keep=0):
        done = sent[: len(sent) - keep]
        del sent[: len(done)]
        for cp in done:
            cp.wait_send()

    def send(src, dst, ss, rs, dev):
        cp = pltpu.make_async_remote_copy(
            src_ref=src, dst_ref=dst, send_sem=ss, recv_sem=rs, device_id=dev, device_id_type=MESH
        )
        cp.start()
        sent.append(cp)
        return cp

    loads = [
        pltpu.make_async_copy(src, dst, loc_sem.at[i])
        for i, (src, dst) in enumerate((
            (tok_hbm, tok_ref), (down_hbm, down_ref), (up_hbm, up_ref), (scale_hbm, scale_ref),
            (codes_hbm, codes), (ub_hbm, ub), (hg_hbm, hg),
        ))
    ]
    barrier = pltpu.get_barrier_semaphore()
    greet = [zid(k) for k in PEERS] + [yid(k) for k in PEERS] + [xid(k) for k in (2, 1, 3)] + [sib]
    for dev in greet:
        pl.semaphore_signal(barrier, inc=1, device_id=dev, device_id_type=MESH)
    for ld in loads:
        ld.start()
    loads[0].wait()

    def piece(rel):
        o = owner(rel)
        two = tok_ref[:, pl.ds(pl.multiple_of((o // 2) * 128, 128), 128)].astype(f32)
        return jnp.where(lax.rem(o, 2) == 1, two[:, 64:], two[:, :64])

    for j, rel in ((0, 4), (1, 0)):
        p = piece(rel)
        PK[j, z, c] = jnp.concatenate([p[:32], p[32:]], axis=1).astype(bf16)
    for b in (1, 2, 3):
        G[b, z, c] = jnp.concatenate([piece(4 - b), piece(4 + b)], axis=1).astype(bf16)
    pl.semaphore_wait(barrier, len(greet))

    def tokens_of(item):
        return PK.at[item // 4] if item in (0, 4) else G.at[item]

    tok = {}

    def spread(item):
        ref = tokens_of(item).at[z, c]
        for k in PEERS:
            tok[item, k] = send(ref, ref, tok_s.at[item, k - 1], tok_r.at[item, k - 1], zid(k))

    spread(0)

    for ld in loads[1:5]:
        ld.wait()
    scale[...] = scale_ref[...].astype(f32)

    def weight_block(i):
        rows = pl.ds(pl.multiple_of(i * 128, 128), 128)
        dn = down_ref[:, rows].astype(f32).T
        dn2 = (2.0 * dn).astype(bf16)
        for lo, hi in ((0, 512), (512, 1024), (1024, 1664)):
            low = jnp.dot(dn2, up_ref[:, lo:hi], preferred_element_type=f32)
            w = codes[rows, lo:hi].astype(f32) * scale[pl.ds(i, 1), lo:hi] + low
            W[i, :, :, lo:hi] = w.astype(bf16).reshape(2, PD, hi - lo)
        WA[i] = jnp.concatenate([dn, jnp.zeros_like(dn)], axis=1).astype(bf16).reshape(2, PD, 128)

    pl.loop(0, NZ // 2)(weight_block)
    spread(1)
    pl.loop(NZ // 2, NZ)(weight_block)
    for item in (2, 3, 4):
        spread(item)

    fwd = {}

    def forward(item):
        for k in PEERS:
            tok[item, k].wait_recv()
        ref = tokens_of(item).at[:, c]
        fwd[item] = send(ref, ref, sib_s.at[item], sib_r.at[item], sib)

    def landed(item):
        fwd[item].wait_recv()
        if item in (0, 4):
            xt[:, :512] = PK[item // 4].reshape(512, 128).T
        else:
            xt[...] = G[item].reshape(D, 128).T

    def times(item, w, lo, hi):
        if item in (0, 4):
            return jnp.dot(
                xt[:64, :512], w[:, :, :32, lo:hi].reshape(512, hi - lo), preferred_element_type=f32
            ) + jnp.dot(
                xt[64:, :512], w[:, :, 32:, lo:hi].reshape(512, hi - lo), preferred_element_type=f32
            )
        return jnp.dot(xt[...], w[:, :, :, lo:hi].reshape(D, hi - lo), preferred_element_type=f32)

    def rels(item):
        return (4 - item,) if item in (0, 4) else (4 - item, 4 + item)

    def gemm1(item, q):
        lo, hi = CHUNKS[q]
        p = times(item, W, lo, hi)
        for i, rel in enumerate(rels(item)):
            part[rel, :, lo:hi] = p[64 * i : 64 * i + 64]

    def gemm_a(item):
        p = times(item, WA, 0, 128)
        for i, rel in enumerate(rels(item)):
            part_a[rel] = p[64 * i : 64 * i + 64]

    def packed(rel):
        v = part_a[rel, pl.ds(pl.multiple_of(c * 32, 32), 32), :]
        return v[:16] + jnp.concatenate([v[16:, 64:], v[16:, :64]], axis=1)

    rs = {}

    def rs_step(step, q):
        lo, hi = CHUNKS[q]
        for d, sign in ((0, 1), (1, -1)):
            rel = (sign * (5 - step)) % 8
            half = slice(0, 32) if d == 0 else slice(32, 64)
            other = slice(32, 64) if d == 0 else slice(0, 32)
            dst = rs_snd.at[d, step - 1]
            if step == 1:
                rs_snd[d, 0, half, lo:hi] = part[rel, half, lo:hi].astype(bf16)
                src, tgt = dst.at[half, lo:hi], rs_rcv.at[d, 0, half, lo:hi]
            else:
                rs[d, step - 1, q].wait_recv()
                if step == 2:
                    rs_snd[d, 1, half, lo:hi] = (
                        part[rel, half, lo:hi] + rs_rcv[d, 0, half, lo:hi].astype(f32)
                    ).astype(bf16)
                    rs_snd[d, 1, other, lo:hi] = part[rel, other, lo:hi].astype(bf16)
                else:
                    rs_snd[d, step - 1, :, lo:hi] = (
                        part[rel, :, lo:hi] + rs_rcv[d, step - 2, :, lo:hi].astype(f32)
                    ).astype(bf16)
                src, tgt = dst.at[:, lo:hi], rs_rcv.at[d, step - 1, :, lo:hi]
            rs[d, step, q] = send(
                src, tgt, rs_s.at[d, step - 1, q], rs_r.at[d, step - 1, q], yid(sign)
            )

    ra = {}

    def rs_a(step):
        for d, sign in ((0, 1), (1, -1)):
            if d == 1 and step == 1:
                continue
            v = packed((sign * (5 - step)) % 8)
            if step > 1 + d:
                ra[d, step - 1].wait_recv()
                v = v + a_rcv[d, step - 2].astype(f32)
            a_snd[d, step - 1] = v.astype(bf16)
            ra[d, step] = send(
                a_snd.at[d, step - 1], a_rcv.at[d, step - 1],
                ra_s.at[d, step - 1], ra_r.at[d, step - 1], yid(sign),
            )

    def sum_a():
        ra[0, 4].wait_recv()
        ra[1, 4].wait_recv()
        GA[y] = (packed(0) + a_rcv[0, 3].astype(f32) + a_rcv[1, 3].astype(f32)).astype(bf16)

    ga = {}

    def ag_a(hop):
        for d, sign in ((0, 1), (1, -1)):
            if hop > 1:
                ga[d, hop - 1].wait_recv()
            if d == 1 and hop == 4:
                continue
            ref = GA.at[owner((-sign * (hop - 1)) % 8)]
            ga[d, hop] = send(ref, ref, ga_s.at[d, hop - 1], ga_r.at[d, hop - 1], yid(sign))

    def gating(q):
        lo, hi = CHUNKS[q]
        rs[0, 4, q].wait_recv()
        rs[1, 4, q].wait_recv()
        total = part[0, :, lo:hi] + rs_rcv[0, 3, :, lo:hi].astype(f32) + rs_rcv[1, 3, :, lo:hi].astype(f32)
        s = jax.nn.sigmoid(total)
        product = hg[:, lo:hi].astype(f32) * ub[:, lo:hi].astype(f32)
        GR[y, :, lo:hi] = (product * s * (1.0 + total * (1.0 - s))).astype(bf16)

    ag = {}

    def ag_hop(hop, q):
        lo, hi = CHUNKS[q]
        for d, sign in ((0, 1), (1, -1)):
            if hop > 1:
                ag[d, hop - 1, q].wait_recv()
            o = owner((-sign * (hop - 1)) % 8)
            rows = slice(0, 64)
            if hop == 4:
                rows = slice(0, 32) if d == 0 else slice(32, 64)
            ref = GR.at[o, rows, lo:hi]
            ag[d, hop, q] = send(ref, ref, ag_s.at[d, hop - 1, q], ag_r.at[d, hop - 1, q], yid(sign))

    bp, zb, yb = [], {}, {}

    def back_own():
        bk = lax.dot_general(up_ref[...], GR[y], NT, preferred_element_type=f32)
        bk_snd[...] = 2.0 * bk
        bp.append(send(bk_snd, bk_rcv, bp_s, bp_r, sib))

    def back_z():
        bp[0].wait_recv()
        bz_snd[...] = (bk_snd[...] + bk_rcv[...]).reshape(NZ, 8, OWN)
        for k in PEERS:
            zb[k] = send(
                bz_snd.at[lax.rem(z + k, NZ)], bz_rcv.at[k - 1], bz_s.at[k - 1], bz_r.at[k - 1], zid(k)
            )

    def back_y():
        total = bz_snd[z]
        for k in PEERS:
            zb[k].wait_recv()
            total = total + bz_rcv[k - 1]
        by_snd[...] = total
        for k in PEERS:
            yb[k] = send(by_snd, by_rcv.at[k - 1], by_s.at[k - 1], by_r.at[k - 1], yid(k))

    def back_end():
        for k in (0,) + PEERS:
            if k:
                yb[k].wait_recv()
            b, h = block_of((8 - k) % 8)
            back[b, :, h * 64 : h * 64 + 64] = by_rcv[k - 1] if k else by_snd[...]

    pair, zs = {}, {}

    def bufs(g):
        return group_bufs[6 * g : 6 * g + 6]

    def group_add(g, q):
        lo, hi = CHUNKS[q]
        n = 64 * len(GROUPS[g])
        gr = jnp.concatenate([GR[owner(rel), :, lo:hi] for rel in GROUPS[g]], axis=0)
        for ref, core in zip(bufs(g)[4:], (1 - c, c)):
            term = lax.dot_general(
                W[:, core, :, lo:hi].reshape(512, hi - lo), gr, NT, preferred_element_type=f32
            ).reshape(NZ, PD, n)
            ref[...] = term if q == 0 else ref[...] + term

    def compact(g, v):
        return jnp.concatenate([v[:, :32], v[:, 32:]], axis=2) if g == 3 else v

    def group_pair(g):
        psnd, prcv = bufs(g)[:2]
        psnd[...] = compact(g, bufs(g)[4][...]).astype(bf16)
        pair[g] = send(psnd, prcv, p_s.at[g], p_r.at[g], sib)

    def group_own(g):
        _, prcv, zsnd, zrcv, _, own = bufs(g)
        pair[g].wait_recv()
        zsnd[...] = (compact(g, own[...]) + prcv[...].astype(f32)).astype(bf16)
        for k in PEERS:
            zs[g, k] = send(
                zsnd.at[lax.rem(z + k, NZ)], zrcv.at[k - 1], z_s.at[g, k - 1], z_r.at[g, k - 1], zid(k)
            )

    def group_end(g):
        zsnd, zrcv = bufs(g)[2:4]
        total = zsnd[z].astype(f32)
        for k in PEERS:
            zs[g, k].wait_recv()
            total = total + zrcv[k - 1].astype(f32)
        if g == 3:
            zfin[4, :32] = total[:, :64]
            zfin[4, 32:] = total[:, 64:]
            return
        for i, rel in enumerate(GROUPS[g]):
            zfin[rel] = total[:, i * 64 : i * 64 + 64]

    gds = []

    def down_grad():
        back_end()
        gd = jnp.zeros((8, D), f32)
        for b in range(4):
            gd = gd + lax.dot_general(
                back[b].astype(bf16), G[b].reshape(D, 128), NT, preferred_element_type=f32
            )
        gd_all[x] = jnp.where(c == 0, gd[:4], gd[4:]) * (1.0 / 2048.0)
        for k in (2, 1, 3):
            gds.append(send(gd_all.at[x], gd_all.at[x], gd_s.at[k - 1], gd_r.at[k - 1], xid(k)))

    forward(0)
    landed(0)
    for i, q in enumerate(RS_ORDER):
        gemm1(0, q)
        rs_step(1, q)
        if i == 1:
            gemm_a(0)
            rs_a(1)
    for step in (2, 3, 4):
        if step == 2:
            forward(1)
        landed(step - 1)
        for q in RS_ORDER:
            gemm1(step - 1, q)
        gemm_a(step - 1)
        forward(step)
        for i, q in enumerate(RS_ORDER):
            rs_step(step, q)
            if i == 1:
                rs_a(step)
    landed(4)
    for q in RS_ORDER:
        gemm1(4, q)
    gemm_a(4)
    loads[5].wait()
    loads[6].wait()

    gating(4)
    for q in range(Q):
        if q < 4:
            gating(q)
        ag_hop(1, q)
        if q == 0:
            sum_a()
            ag_a(1)
    back_own()
    drain(19)
    low, high = [
        jnp.concatenate([PK[0, :, :, :, h].astype(f32), PK[1, :, :, :, h].astype(f32)], axis=3).astype(bf16)
        for h in (slice(0, 64), slice(64, 128))
    ]
    G[0, :, :, :32, :] = low
    G[0, :, :, 32:, :] = high
    for hop, g in ((2, 0), (3, 1), (4, 2)):
        for q in range(Q):
            ag_hop(hop, q)
            if q == 0:
                ag_a(hop)
            group_add(g, q)
            if g > 0 and q == 0:
                group_own(g - 1)
            if g == 0 and q == 1:
                back_z()
            if g == 1 and q == 2:
                back_y()
            if g == 2 and q == 3:
                down_grad()
        group_pair(g)

    xs, xg = {}, {}

    def last(q):
        ag[0, 4, q].wait_recv()
        ag[1, 4, q].wait_recv()

    def up_part(q):
        lo, hi = CHUNKS[q]
        u = jnp.dot(at_ref[...], GR[:, :, lo:hi].reshape(512, hi - lo), preferred_element_type=f32)
        u = u * (2.0 / 2048.0)
        if q >= TWO:
            up_all[x, :, lo - SPLIT : hi - SPLIT] = u.astype(bf16)
            ref = up_all.at[x, :, lo - SPLIT : hi - SPLIT]
            for k in (2, 1, 3):
                xs[k, q] = send(ref, ref, xs_s.at[k - 1, q], xs_r.at[k - 1, q], xid(k))
            return
        u = u.reshape(NX, 16, hi - lo)
        up_acc[:, :, lo:hi] = u
        xs_snd[:, :, lo:hi] = u.astype(bf16)
        for k in (2, 1, 3):
            xs[k, q] = send(
                xs_snd.at[lax.rem(x + k, NX), :, lo:hi], xs_rcv.at[k - 1, :, lo:hi],
                xs_s.at[k - 1, q], xs_r.at[k - 1, q], xid(k),
            )

    def up_sum(q):
        lo, hi = CHUNKS[q]
        total = up_acc[x, :, lo:hi]
        for k in (1, 2, 3):
            xs[k, q].wait_recv()
            total = total + xs_rcv[k - 1, :, lo:hi].astype(f32)
        xg_snd[:, lo:hi] = total.astype(bf16)
        for k in (2, 1, 3):
            xg[k, q] = send(
                xg_snd.at[:, lo:hi], xg_rcv.at[k - 1, :, lo:hi],
                xg_s.at[k - 1, q], xg_r.at[k - 1, q], xid(k),
            )

    ga[0, 4].wait_recv()
    swap = send(GA, GB, ab_s, ab_r, sib)
    last(0)
    group_add(3, 0)
    group_own(2)
    swap.wait_recv()
    for half, src in ((c, GA), (1 - c, GB)):
        v = src[...].astype(f32)
        a_all[:, 2 * half] = v[:, :, :64]
        a_all[:, 2 * half + 1] = v[:, :, 64:]
    at_ref[...] = a_all[...].reshape(512, R).T.astype(bf16)
    up_part(0)
    for q in range(1, Q):
        last(q)
        group_add(3, q)
        if q < Q - 1:
            up_part(q)
    group_pair(3)
    up_part(Q - 1)
    group_own(3)

    for q in range(TWO):
        up_sum(q)
    group_end(0)
    group_end(1)

    group_end(2)
    drain(24)
    group_end(3)
    for i in range(4):
        a = zfin[lax.rem(2 * i - y + NY, NY)]
        b = zfin[lax.rem(2 * i + 1 - y + NY, NY)]
        out_ref[:, i * 128 : i * 128 + 128] = jnp.concatenate([a, b], axis=1).astype(bf16)

    for q in range(TWO, Q):
        for k in (1, 2, 3):
            xs[k, q].wait_recv()
    gu_ref[:, SPLIT:] = (
        up_all[0].astype(f32) + up_all[1].astype(f32) + up_all[2].astype(f32) + up_all[3].astype(f32)
    )
    for q in range(TWO):
        for k in (1, 2, 3):
            xg[k, q].wait_recv()
    gu_ref[pl.ds(pl.multiple_of(x * 16, 16), 16), :SPLIT] = xg_snd[...].astype(f32)
    for k in (1, 2, 3):
        at = pl.multiple_of(lax.rem(x - k + NX, NX) * 16, 16)
        gu_ref[pl.ds(at, 16), :SPLIT] = xg_rcv[k - 1].astype(f32)
    for cp in gds:
        cp.wait_recv()
    gd_ref[...] = gd_all[0] + gd_all[1] + gd_all[2] + gd_all[3]
    drain()


def finish(out_ref, gd_ref, gu_ref, out_hbm, gd_hbm, gu_hbm, sem):
    copies = [
        pltpu.make_async_copy(src, dst, sem.at[i])
        for i, (src, dst) in enumerate(((gu_ref, gu_hbm), (out_ref, out_hbm), (gd_ref, gd_hbm)))
    ]
    for cp in copies:
        cp.start()
    for cp in copies:
        cp.wait()


def group_scratch(n):
    d, t = (PD // 2, 128) if n == 64 else (PD, n)
    return [
        pltpu.VMEM((NZ, d, t), bf16),
        pltpu.VMEM((NZ, d, t), bf16),
        pltpu.VMEM((NZ, d, t), bf16),
        pltpu.VMEM((NZ - 1, d, t), bf16),
        pltpu.VMEM((NZ, PD, n), f32),
        pltpu.VMEM((NZ, PD, n), f32),
    ]


def per_device(tokens, codes, scales, down, up, up_branch, hidden_grad):
    vmem = pl.BlockSpec(memory_space=pltpu.VMEM)
    hbm = pl.BlockSpec(memory_space=pl.ANY)
    dma = pltpu.SemaphoreType.DMA
    scratch = [
        pltpu.VMEM((PD, 512), bf16),
        pltpu.VMEM((D, F), bf16),
        pltpu.VMEM((8, F), bf16),
        pltpu.VMEM((R, D), bf16),
        pltpu.VMEM((R, F), bf16),
        pltpu.VMEM((OWN, F), bf16),
        pltpu.VMEM((OWN, F), bf16),
        pltpu.VMEM((8, F), f32),
        pltpu.VMEM((NZ, 2, PD, F), bf16),
        pltpu.VMEM((NZ, 2, PD, 128), bf16),
        pltpu.VMEM((4, NZ, 2, PD, 128), bf16),
        pltpu.VMEM((2, NZ, 2, PD // 2, 128), bf16),
        pltpu.VMEM((128, D), bf16),
        pltpu.VMEM((NY, OWN, F), f32),
        pltpu.VMEM((NY, OWN, 128), f32),
        pltpu.VMEM((2, 4, OWN, F), bf16),
        pltpu.VMEM((2, 4, OWN, F), bf16),
        pltpu.VMEM((2, 4, 16, 128), bf16),
        pltpu.VMEM((2, 4, 16, 128), bf16),
        pltpu.VMEM((NY, OWN, F), bf16),
        pltpu.VMEM((NY, 16, 128), bf16),
        pltpu.VMEM((NY, 16, 128), bf16),
        pltpu.VMEM((NY, 4, 16, R), f32),
        pltpu.VMEM((4, 8, 128), f32),
        pltpu.VMEM((R, OWN), f32),
        pltpu.VMEM((R, OWN), f32),
        pltpu.VMEM((NZ, 8, OWN), f32),
        pltpu.VMEM((NZ - 1, 8, OWN), f32),
        pltpu.VMEM((8, OWN), f32),
        pltpu.VMEM((NY - 1, 8, OWN), f32),
        pltpu.VMEM((NY, PD, OWN), f32),
        pltpu.VMEM((R, 512), bf16),
        pltpu.VMEM((NX, 16, SPLIT), f32),
        pltpu.VMEM((NX, R, F - SPLIT), bf16),
        pltpu.VMEM((NX, 16, SPLIT), bf16),
        pltpu.VMEM((NX - 1, 16, SPLIT), bf16),
        pltpu.VMEM((16, SPLIT), bf16),
        pltpu.VMEM((NX - 1, 16, SPLIT), bf16),
        pltpu.VMEM((NX, 4, D), f32),
    ]
    for g in GROUPS:
        scratch += group_scratch(64 * len(g))
    scratch += [
        dma((7,)),
        dma((5, 7)), dma((5, 7)),
        dma((5,)), dma((5,)),
        dma((2, 4, Q)), dma((2, 4, Q)),
        dma((2, 4, Q)), dma((2, 4, Q)),
        dma((2, 4)), dma((2, 4)),
        dma((2, 4)), dma((2, 4)),
        dma, dma,
        dma((4,)), dma((4,)),
        dma((4, 7)), dma((4, 7)),
        dma, dma,
        dma((7,)), dma((7,)),
        dma((7,)), dma((7,)),
        dma((3, Q)), dma((3, Q)),
        dma((3, Q)), dma((3, Q)),
        dma((3,)), dma((3,)),
    ]
    shapes = (((PD, 512), bf16), ((4, D), f32), ((R, F), f32))
    parts = pl.pallas_call(
        kernel,
        out_shape=tuple(pltpu.VMEM(*s) for s in shapes),
        in_specs=[hbm] * 7,
        out_specs=(vmem,) * 3,
        scratch_shapes=scratch,
        compiler_params=pltpu.CompilerParams(
            collective_id=0, has_side_effects=True, vmem_limit_bytes=56 << 20
        ),
    )(tokens.T, codes, scales, down.T, up, up_branch, hidden_grad)
    out_t, gd_t, gu = pl.pallas_call(
        finish,
        out_shape=tuple(jax.ShapeDtypeStruct(*s) for s in shapes),
        in_specs=[hbm] * 3,
        out_specs=(hbm,) * 3,
        scratch_shapes=[dma((3,))],
    )(*(pltpu.with_memory_space_constraint(a, pltpu.VMEM) for a in parts))
    return out_t.T, gd_t.T, gu


def solution(mesh):
    return jax.shard_map(
        per_device,
        mesh=mesh,
        in_specs=(
            P("dp", ("row", "col")),
            P("row", "col"),
            P("row", "col"),
            P("row", None),
            P(None, "col"),
            P(("dp", "row"), "col"),
            P(("dp", "row"), "col"),
        ),
        out_specs=(P("dp", ("row", "col")), P("row", "col"), P(None, "col")),
        check_vma=False,
    )
```

profile of v0, /device:TPU:1, one launch (start us, length us, event | category | flops | bytes accessed | tf_op | source)
XLA Modules:
  0.0 73.4 jit_solution(70031001209194613)
XLA Ops:
  0.6 71.9 %shard_map.94 = (bf16[64,512]{1,0:T(8,128)(2,1)S(1)}, f32[4,1024]{1,0:T(4,128)S(1)}, f32[64,1664]{1,0:T(8,128)S(1)}) custom-call(bf16[64,512]{1,0:T(8,128)(2,1)} %bitcast.5, bf16[1024,1664]{1,0:T(8,128)(2,1)} %codes_hbm.1, bf16[8,1664]{1,0:T(8,128)(2,1)} %scale_hbm.1, bf16[64,1024]{1,0:T(8,128)(2,1)} %bitcast.4, bf16[64,1664]{1,0:T(8,128)(2,1)} %up_hbm.1, ...), custom_call_target="tpu_custom_call" | custom-call | tf_op jit(solution)/shard_map/pallas_call | solution.py:592
  72.6 0.8 %shard_map.95 = (bf16[64,512]{1,0:T(8,128)(2,1)}, f32[4,1024]{1,0:T(4,128)}, f32[64,1664]{1,0:T(8,128)}) custom-call(bf16[64,512]{1,0:T(8,128)(2,1)S(1)} %get-tuple-element.9.out_ref, f32[4,1024]{1,0:T(4,128)S(1)} %get-tuple-element.10.gd_ref, f32[64,1664]{1,0:T(8,128)S(1)} %get-tuple-element.11.gu_ref), custom_call_target="tpu_custom_call" | custom-call | tf_op jit(solution)/shard_map/pallas_call | solution.py:602
where the time goes:
time: 73.5 us; the launch traced here: 73.4 us
  Pallas kernels  72.7 us (99%)
    pallas_call x1, Pallas kernels, per_device(): pl.pallas_call(kernel, out_shape=tuple((pltpu.VMEM(*s) for s in shapes)),...  71.9 us

commit v1 on v0

--- a/solution.py
+++ b/solution.py
@@ -281,7 +281,7 @@
         for k in PEERS:
             zb[k].wait_recv()
             total = total + bz_rcv[k - 1]
-        by_snd[...] = total
+        by_snd[...] = jnp.where(c == 0, total[:4], total[4:])
         for k in PEERS:
             yb[k] = send(by_snd, by_rcv.at[k - 1], by_s.at[k - 1], by_r.at[k - 1], yid(k))
 
@@ -341,12 +341,12 @@
 
     def down_grad():
         back_end()
-        gd = jnp.zeros((8, D), f32)
+        gd = jnp.zeros((4, D), f32)
         for b in range(4):
             gd = gd + lax.dot_general(
                 back[b].astype(bf16), G[b].reshape(D, 128), NT, preferred_element_type=f32
             )
-        gd_all[x] = jnp.where(c == 0, gd[:4], gd[4:]) * (1.0 / 2048.0)
+        gd_all[x] = gd * (1.0 / 2048.0)
         for k in (2, 1, 3):
             gds.append(send(gd_all.at[x], gd_all.at[x], gd_s.at[k - 1], gd_r.at[k - 1], xid(k)))
 
@@ -551,13 +551,13 @@
         pltpu.VMEM((NY, 16, 128), bf16),
         pltpu.VMEM((NY, 16, 128), bf16),
         pltpu.VMEM((NY, 4, 16, R), f32),
-        pltpu.VMEM((4, 8, 128), f32),
+        pltpu.VMEM((4, 4, 128), f32),
         pltpu.VMEM((R, OWN), f32),
         pltpu.VMEM((R, OWN), f32),
         pltpu.VMEM((NZ, 8, OWN), f32),
         pltpu.VMEM((NZ - 1, 8, OWN), f32),
-        pltpu.VMEM((8, OWN), f32),
-        pltpu.VMEM((NY - 1, 8, OWN), f32),
+        pltpu.VMEM((4, OWN), f32),
+        pltpu.VMEM((NY - 1, 4, OWN), f32),
         pltpu.VMEM((NY, PD, OWN), f32),
         pltpu.VMEM((R, 512), bf16),
         pltpu.VMEM((NX, 16, SPLIT), f32),

time: 73.5 us -> 73.1 us (level)
  no operation moved by 1% of the time
where the time goes in v1:
time: 73.1 us; the launch traced here: 73 us
  Pallas kernels  72.4 us (99%)
    pallas_call x1, Pallas kernels, per_device(): pl.pallas_call(kernel, out_shape=tuple((pltpu.VMEM(*s) for s in shapes)),...  71.6 us

profile of v1, /device:TPU:1, one launch (start us, length us, event | category | flops | bytes accessed | tf_op | source)
XLA Modules:
  0.0 73.0 jit_solution(11865612839430700247)
XLA Ops:
  0.6 71.6 %shard_map.94 = (bf16[64,512]{1,0:T(8,128)(2,1)S(1)}, f32[4,1024]{1,0:T(4,128)S(1)}, f32[64,1664]{1,0:T(8,128)S(1)}) custom-call(bf16[64,512]{1,0:T(8,128)(2,1)} %bitcast.5, bf16[1024,1664]{1,0:T(8,128)(2,1)} %codes_hbm.1, bf16[8,1664]{1,0:T(8,128)(2,1)} %scale_hbm.1, bf16[64,1024]{1,0:T(8,128)(2,1)} %bitcast.4, bf16[64,1664]{1,0:T(8,128)(2,1)} %up_hbm.1, ...), custom_call_target="tpu_custom_call" | custom-call | tf_op jit(solution)/shard_map/pallas_call | solution.py:592
  72.2 0.8 %shard_map.95 = (bf16[64,512]{1,0:T(8,128)(2,1)}, f32[4,1024]{1,0:T(4,128)}, f32[64,1664]{1,0:T(8,128)}) custom-call(bf16[64,512]{1,0:T(8,128)(2,1)S(1)} %get-tuple-element.9.out_ref, f32[4,1024]{1,0:T(4,128)S(1)} %get-tuple-element.10.gd_ref, f32[64,1664]{1,0:T(8,128)S(1)} %get-tuple-element.11.gu_ref), custom_call_target="tpu_custom_call" | custom-call | tf_op jit(solution)/shard_map/pallas_call | solution.py:602
